TPU v7x, 128 devices: a whole 4x4x4 slice. The times are simulated.
128 devices in a mesh: ep: 32 (over y, z, core), tp: 4 (over x).
Axes of the slice: x: 4, y: 4, z: 4, core: 2. Of those that a mesh axis runs over, the one named last changes fastest.
Arguments:
- queries: bfloat16 [256, 64, 128], P('ep', 'tp'), may hold values from -115 to 115
- key_cache: bfloat16 [256, 4, 1024, 128], P('ep', 'tp'), may hold values from -6 to 6
- stored_value_cache: bfloat16 [256, 4, 1024, 128], P('ep', 'tp'), may hold values from -6 to 6
- new_key: bfloat16 [256, 4, 128], P('ep', 'tp'), may hold values from -4.5 to 4.5
- incoming_value: bfloat16 [256, 4, 128], P('ep', 'tp'), may hold values from -6 to 6
- lengths: int32 [256], P('ep'), may hold values from 1 to 1024, as said below
- policy: int32 [256, 4], P('ep', 'tp'), may hold values from 0 to 2
- retained_blocks: int32 [256, 4, 4], P('ep', 'tp'), may hold values from 0 to 15
- out_weight: bfloat16 [8192, 4096], P(None, 'ep'), may hold values from -0.5 to 0.5
- residual: bfloat16 [256, 4096], P(None, 'ep'), may hold values from -6 to 6
- norm_gain: float32 [4096], replicated, may hold values from 0.1 to 1.9
- routes: int32 [256, 8], replicated, may hold values from 0 to 63, all different within a row; in each aligned block of 256 rows (0 to 255, 256 to 511, ...) at most 64 rows name the same one
- router_logits: float32 [256, 8], replicated, may hold values from -6 to 6
- gate_weight: bfloat16 [64, 4096, 1536], P('ep', None, 'tp'), may hold values from -0.09375 to 0.09375
- up_weight: bfloat16 [64, 4096, 1536], P('ep', None, 'tp'), may hold values from -0.09375 to 0.09375
- down_weight: bfloat16 [64, 1536, 4096], P('ep', 'tp'), may hold values from -0.15625 to 0.15625
Outputs:
- mixed_out: bfloat16 [256, 4096], P(None, ('ep', 'tp'))
Inputs may be any that keep to these rules, and one draw needn't show every extreme that they name: `lengths`: each aligned group of 8 requests holds one of length 1024. At most 64 of all routes name one expert, a bound that some block reaches; a token names 8 different experts.
All inputs are finite; a program needn't handle non-finite values.
Results may differ from a plain program's by a relative error of at most 0.015.
Values may be sent and summed in bfloat16 or wider, within the bound.
A program may use at most 128 MiB of HBM per device.

v0:
```python
import jax
import jax.numpy as jnp
from jax import lax
from jax.sharding import PartitionSpec as P

TOPK = 8
EXP_DEV = 2
BLK = 64
BLOCK_COUNT = 16
WIN = 2
CONTEXT_SLOTS = 1024
CAP = 64


EPSILON = 1e-06


def token_keep(policy, retained_blocks, lengths):
    block_ids = jnp.arange(BLOCK_COUNT, dtype=jnp.int32)
    used_count = (lengths + BLK - 1) // BLK
    used_mask = block_ids < used_count[..., None]
    recent = block_ids >= (used_count - WIN)[..., None]
    last_block = block_ids == (used_count - 1)[..., None]
    listed = jnp.any(retained_blocks[..., :, None] == block_ids, axis=-2)
    policy_col = policy[..., None]
    block_keep = used_mask & (
        (policy_col == 0) & recent | (policy_col == 1) & (listed | last_block) | (policy_col == 2)
    )
    positions = jnp.arange(CONTEXT_SLOTS, dtype=jnp.int32)
    return jnp.repeat(block_keep, BLK, axis=-1) & (positions < lengths[..., None])


def per_device(
    queries,
    key_cache,
    stored_value_cache,
    new_key,
    incoming_value,
    lengths,
    policy,
    retained_blocks,
    out_weight,
    residual,
    norm_gain,
    routes,
    router_logits,
    gate_weight,
    up_weight,
    down_weight,
):
    ep_count = lax.axis_size("ep")
    tp_count = lax.axis_size("tp")
    request_count = queries.shape[0]
    group_heads = queries.shape[1]
    head_size = queries.shape[2]
    head_width = group_heads * head_size
    score_scale = head_size ** (-0.5)
    key_rows = key_cache[:, 0]
    value_rows = stored_value_cache[:, 0]
    own_key = new_key[:, 0]
    own_value = incoming_value[:, 0]
    kept_mask = token_keep(policy[:, 0], retained_blocks[:, 0], lengths)
    own_score = (
        jnp.einsum("rqd,rd->rq", queries, own_key, preferred_element_type=jnp.float32) * score_scale
    )
    scores = (
        jnp.einsum("rqd,rkd->rqk", queries, key_rows, preferred_element_type=jnp.float32)
        * score_scale
    )
    scores = jnp.where(kept_mask[:, None, :], scores, -jnp.inf)
    highest = jnp.maximum(jnp.max(scores, axis=-1), own_score)
    weights = jnp.exp(scores - highest[..., None])
    own_weight = jnp.exp(own_score - highest)
    totals = jnp.sum(weights, axis=-1) + own_weight
    own_low = lax.optimization_barrier(own_weight.astype(jnp.bfloat16)).astype(jnp.float32)
    weighted = jnp.einsum(
        "rqk,rkd->rqd", weights.astype(jnp.bfloat16), value_rows, preferred_element_type=jnp.float32
    )
    weighted = weighted + own_low[..., None] * own_value.astype(jnp.float32)[:, None, :]
    attended = (
        (weighted / totals[..., None]).astype(jnp.bfloat16).reshape(1, request_count, head_width)
    )
    column_count = out_weight.shape[1]
    all_requests = request_count * ep_count
    weight_parts = out_weight.reshape(tp_count, head_width, column_count)
    group_ids = jnp.arange(ep_count, dtype=jnp.int32)
    head_ids = jnp.arange(tp_count, dtype=jnp.int32)
    shard_rows = lax.all_gather(attended, ("ep", "tp"), axis=0, tiled=True)
    device_ids = jnp.arange(shard_rows.shape[0], dtype=jnp.int32)
    terms = jnp.einsum(
        "srk,tkc->strc", shard_rows, weight_parts, preferred_element_type=jnp.float32
    )
    head_match = (device_ids % tp_count)[:, None] == head_ids[None, :]
    chosen = jnp.sum(jnp.where(head_match[:, :, None, None], terms, 0.0), axis=1)
    group_match = (device_ids // tp_count)[:, None] == group_ids[None, :]
    added = jnp.sum(jnp.where(group_match[:, :, None, None], chosen[:, None], 0.0), axis=0)
    projected = added.reshape(all_requests, column_count)
    hidden = (residual.astype(jnp.float32) + projected).astype(jnp.bfloat16)
    experts_all = EXP_DEV * ep_count
    route_flat = routes.reshape(-1)
    onehot = (route_flat[:, None] == jnp.arange(experts_all, dtype=jnp.int32)[None, :]).astype(
        jnp.int32
    )
    route_rank = jnp.sum(jnp.cumsum(onehot, axis=0) * onehot, axis=1) - 1
    slot_index = route_flat * CAP + route_rank
    token_index = jnp.arange(route_flat.shape[0], dtype=jnp.int32) // TOPK
    outgoing_rows = (
        jnp.zeros((experts_all * CAP, column_count), jnp.bfloat16)
        .at[slot_index]
        .set(hidden[token_index])
    )
    arrived = lax.all_to_all(outgoing_rows, "ep", split_axis=0, concat_axis=1, tiled=True)
    rows_float = arrived.astype(jnp.float32)
    normed = (
        rows_float
        * lax.rsqrt(jnp.mean(rows_float * rows_float, axis=-1, keepdims=True) + EPSILON)
        * norm_gain
    ).astype(jnp.bfloat16)
    normed = normed.reshape(EXP_DEV, CAP, normed.shape[1])
    gate = jnp.einsum("ecd,edf->ecf", normed, gate_weight, preferred_element_type=jnp.float32)
    up_proj = jnp.einsum("ecd,edf->ecf", normed, up_weight, preferred_element_type=jnp.float32)
    act = (jax.nn.silu(gate) * up_proj).astype(jnp.bfloat16)
    partial_value = jnp.einsum("ecf,efd->ecd", act, down_weight, preferred_element_type=jnp.float32)
    partial_value = partial_value.reshape(1, EXP_DEV * CAP, partial_value.shape[2])
    returned = lax.all_to_all(
        lax.all_to_all(
            partial_value.astype(jnp.bfloat16), "ep", split_axis=2, concat_axis=1, tiled=True
        ),
        "tp",
        split_axis=2,
        concat_axis=0,
        tiled=True,
    ).astype(partial_value.dtype)
    summed = jnp.sum(returned, axis=0)
    route_weight = jax.nn.softmax(router_logits, axis=-1)
    narrow = summed.shape[1]
    picked_rows = summed[slot_index].reshape(-1, TOPK, narrow)
    mixture = jnp.sum(picked_rows * route_weight[..., None], axis=1)
    tp_index_out = lax.axis_index("tp")
    base_rows = lax.dynamic_slice_in_dim(hidden, tp_index_out * narrow, narrow, 1)
    return (base_rows.astype(jnp.float32) + mixture).astype(jnp.bfloat16)


def solution(mesh):
    return jax.shard_map(
        per_device,
        mesh=mesh,
        in_specs=(
            P("ep", "tp", None),
            P("ep", "tp", None, None),
            P("ep", "tp", None, None),
            P("ep", "tp", None),
            P("ep", "tp", None),
            P("ep"),
            P("ep", "tp"),
            P("ep", "tp", None),
            P(None, "ep"),
            P(None, "ep"),
            P(),
            P(),
            P(),
            P("ep", None, "tp"),
            P("ep", None, "tp"),
            P("ep", "tp", None),
        ),
        out_specs=P(None, ("ep", "tp")),
        check_vma=False,
    )
```

profile of v0, /device:TPU:1, one launch (start us, length us, event | category | flops | bytes accessed | tf_op | source)
XLA Modules:
  0.0 263.7 jit_solution(4339838347839793135)
XLA Ops:
  6.5 0.8 broadcast_add_fusion.2
  7.4 0.7 compare_bitcast_fusion.2
  8.0 0.8 fusion.44
  9.1 0.9 fusion.43
  10.0 0.9 fusion.47
  10.8 2.4 fusion.58
  15.1 18.1 %reduce-window.6 = s32[64,16,128]{2,1,0:T(8,128)S(1)} reduce-window(s32[64,16,128]{2,1,0:T(8,128)S(1)} %fusion.31, s32[]{:T(128)} %constant.89.clone.1), window={size=1x1x128 pad=0_0x0_0x127_0}, to_apply=%region_5.6 | reduce-window | flops 16646144 | bytes 1048580 | tf_op jit(solution)/shard_map/reduce-window
  35.0 50.4 %all-gather.2.cloned.1.call-done = bf16[128,8,2048]{2,1,0:T(8,128)(2,1)} async-done(((bf16[1,8,2048]{2,1,0:T(8,128)(2,1)}), bf16[128,8,2048]{2,1,0:T(8,128)(2,1)}) %all-gather.2.cloned.1.call-update) | async-done | bytes 4194320 | tf_op jit(solution)/shard_map/all_gather | solution.py:88
  85.4 7.0 %select_reduce_fusion.1 = f32[128,8,128]{2,0,1:T(8,128)S(1)} fusion(bf16[4,2048,128,1]{2,1,0,3:T(8,128)(2,1)S(1)} %bitcast.80, bf16[128,8,2048,1]{2,1,0,3:T(8,128)(2,1)} %bitcast.101, pred[128,4]{0,1:T(4,128)(4,1)S(1)} %iota_compare_fusion.8), kind=kOutput, calls=%fused_computation.16 | convolution fusion | flops 2148401152 | bytes 6816256 | tf_op jit(solution)/shard_map/srk,tkc->strc/dot_general | solution.py:90
  92.7 5.6 %select_reduce_fusion = f32[32,8,128]{2,1,0:T(8,128)S(1)} fusion(f32[128,8,128]{2,1,0:T(8,128)S(1)} %copy.111, pred[128,32]{1,0:T(8,128)(4,1)S(1)} %iota_compare_fusion.2), kind=kLoop, calls=%fused_computation.3 | loop fusion | flops 8355840 | bytes 659456 | tf_op jit(solution)/shard_map/reduce_sum | solution.py:96
  98.5 12.9 %scatter_custom_fusion = bf16[4096,128]{1,0:T(8,128)(2,1)} fusion(s32[2048]{0:T(1024)S(1)} %bitcast.94, bf16[256,128]{1,0:T(8,128)(2,1)S(1)} %copy.118, s32[2048]{0:T(1024)S(1)} %broadcast_clamp_fusion.1, bf16[]{:T(256)} %constant.103.clone.1), kind=kCustom, calls=%fused_computation.29 | custom fusion | bytes 1048578 | tf_op jit(solution)/shard_map/scatter | solution.py:110
  111.4 21.7 %all_to_all.40 = bf16[32,128,128]{2,1,0:T(8,128)(2,1)S(1)} all-to-all(bf16[32,128,128]{2,1,0:T(8,128)(2,1)} %bitcast.89), channel_id=1, replica_groups=mesh['ep'=32,'tp'=4] {'ep'}, dimensions={0} | all-to-all | bytes 2097152 | tf_op jit(solution)/shard_map/all_to_all | solution.py:112
  133.3 2.6 copy.119
  135.9 2.7 %reshape.261 = f32[2,64,4096]{2,1,0:T(8,128)} reshape(f32[128,32,128]{2,1,0:T(8,128)} %copy.119) | data formatting | bytes 4194304 | tf_op jit(solution)/shard_map/convert_element_type | solution.py:113
  139.0 4.5 %fusion.34 = f32[2,64,384]{2,1,0:T(8,128)S(1)} fusion(bf16[2,4096,384]{2,1,0:T(8,128)(2,1)} %param.29, f32[2,64,4096]{2,1,0:T(8,128)} %reshape.261, f32[4096]{0:T(1024)S(1)} %copy-done.2, f32[2,64]{1,0:T(2,128)S(1)} %rsqrt.12), kind=kOutput, calls=%fused_computation.38 | convolution fusion | flops 404226048 | bytes 8602112 | tf_op jit(solution)/shard_map/ecd,edf->ecf/dot_general | solution.py:120
  143.6 7.2 %convolution_convert_fusion = bf16[2,64,4096]{2,1,0:T(8,128)(2,1)S(1)} fusion(bf16[2,384,4096]{2,1,0:T(8,128)(2,1)} %param.31, bf16[2,4096,384]{2,1,0:T(8,128)(2,1)} %param.30, f32[2,64,4096]{2,1,0:T(8,128)} %reshape.261, f32[4096]{0:T(1024)S(1)} %copy-done.2, f32[2,64]{1,0:T(2,128)S(1)} %rsqrt.12, f32[2,64,384]{2,1,0:T(8,128)S(1)} %fusion.34), kind=kOutput, calls=%fused_computation.4 | convolution fusion | flops 807698432 | bytes 15942144 | tf_op jit(solution)/shard_map/ecf,efd->ecd/dot_general | solution.py:123
  150.7 3.9 %copy.120 = bf16[1,128,4096]{1,0,2:T(2,128)(2,1)} copy(bf16[1,128,4096]{2,1,0:T(8,128)(2,1)S(1)} %bitcast.85) | data formatting | bytes 2097152 | tf_op jit(solution)/shard_map/convert_element_type | solution.py:127
  155.1 23.4 %reduce.6 = bf16[4096,128]{1,0:T(8,128)(2,1)S(1)} reduce(bf16[4096,1,128]{2,1,0:T(2,128)(2,1)} %bitcast.83, bf16[]{:T(256)} %broadcast.308), dimensions={1}, to_apply=%bitcast.67.reduce_sub_computation | reduce | bytes 2097154
  178.6 1.1 reshape.297
  179.7 20.9 %all_to_all.41 = bf16[32,2,8192]{2,1,0:T(2,128)(2,1)S(1)} all-to-all(bf16[32,2,8192]{2,1,0:T(2,128)(2,1)} %reshape.297), channel_id=1, replica_groups=mesh['ep'=32,'tp'=4] {'ep'}, dimensions={0} | all-to-all | bytes 2097152 | tf_op jit(solution)/shard_map/all_to_all | solution.py:126
  200.6 3.5 %reshape.298 = bf16[4096,1,128]{2,1,0:T(2,128)(2,1)} reshape(bf16[32,2,8192]{2,1,0:T(2,128)(2,1)S(1)} %all_to_all.41) | data formatting | bytes 2097152
  204.0 1.7 copy.133
  205.7 1.3 copy.121
  207.1 5.5 %copy.122 = bf16[1,4096,128]{1,0,2:T(2,128)(2,1)} copy(bf16[1,4096,128]{2,1,0:T(8,128)(2,1)} %bitcast.87) | data formatting | bytes 2097152 | tf_op jit(solution)/shard_map/all_to_all | solution.py:126
  212.6 8.4 %reduce.7 = bf16[128,4096]{1,0:T(8,128)(2,1)S(1)} reduce(bf16[128,1,4096]{2,1,0:T(2,128)(2,1)} %bitcast.84, bf16[]{:T(256)} %broadcast.308), dimensions={1}, to_apply=%bitcast.69.reduce_sub_computation | reduce | bytes 2097154
  221.0 2.0 reshape.299
  223.0 3.5 %all-to-all-start.2 = ((bf16[4,2,65536]{2,1,0:T(2,128)(2,1)}), bf16[4,2,65536]{2,1,0:T(2,128)(2,1)S(1)}, u32[]{:S(2)}, u32[]{:S(2)}) async-start(bf16[4,2,65536]{2,1,0:T(2,128)(2,1)} %reshape.299), calls=%async_computation.2 | async-start | bytes 2097152 | tf_op jit(solution)/shard_map/all_to_all | solution.py:125
  226.7 14.8 %all-to-all-done.2 = bf16[4,2,65536]{2,1,0:T(2,128)(2,1)S(1)} async-done(((bf16[4,2,65536]{2,1,0:T(2,128)(2,1)}), bf16[4,2,65536]{2,1,0:T(2,128)(2,1)S(1)}, u32[]{:S(2)}, u32[]{:S(2)}) %all-to-all-start.2) | async-done | bytes 1048608 | tf_op jit(solution)/shard_map/all_to_all | solution.py:125
  241.5 2.3 reshape.300
  243.9 2.7 %copy.123 = bf16[1,4096,128]{1,2,0:T(8,128)(2,1)S(1)} copy(bf16[1,4096,128]{1,0,2:T(2,128)(2,1)} %bitcast.82) | data formatting | bytes 2097152 | tf_op jit(solution)/shard_map/all_to_all | solution.py:125
  246.8 2.0 copy.124
  248.7 7.0 %gather_fusion = f32[2048,32]{1,0:T(8,128)S(1)} fusion(f32[4096,32]{1,0:T(8,128)} %copy.124, s32[2048]{0:T(1024)S(1)} %broadcast_clamp_fusion), kind=kCustom, calls=%fused_computation.1 | custom fusion | bytes 532480 | tf_op jit(solution)/shard_map/gather | solution.py:137
  (66 shorter events, 6.8 us)
Async XLA Ops:
  6.5 78.8 %copy-start = (bf16[8192,128]{1,0:T(8,128)(2,1)S(1)}, bf16[8192,128]{1,0:T(8,128)(2,1)}, u32[]{:S(2)}) copy-start(bf16[8192,128]{1,0:T(8,128)(2,1)} %param.24) | copy-start | bytes 6291460
  6.5 6.9 %copy-start.6 = (bf16[8,1,128]{2,0,1:T(8,128)(2,1)S(1)}, bf16[8,1,128]{2,0,1:T(8,128)(2,1)}, u32[]{:S(2)}) copy-start(bf16[8,1,128]{2,0,1:T(8,128)(2,1)} %param.20) | copy-start | bytes 6148
  6.5 78.8 %all-gather.2.cloned.1.call-start = ((), (), s32[]{:S(2)}) async-start(), calls=%async_computation.3 | async-start | bytes 4227072 | tf_op jit(solution)/shard_map/all_gather | solution.py:88
  9.1 4.4 %copy-start.1 = (bf16[8,1,1024,128]{3,2,1,0:T(8,128)(2,1)S(1)}, bf16[8,1,1024,128]{3,2,1,0:T(8,128)(2,1)}, u32[]{:S(2)}) copy-start(bf16[8,1,1024,128]{3,2,1,0:T(8,128)(2,1)} %param.18) | copy-start | bytes 6291460
  13.2 1.4 copy-start.5
  13.2 1.8 copy-start.4
  135.9 3.1 %copy-start.2 = (f32[4096]{0:T(1024)S(1)}, f32[4096]{0:T(1024)}, u32[]{:S(2)}) copy-start(f32[4096]{0:T(1024)} %param.26) | copy-start | bytes 49156
  220.9 5.5 %copy-start.3 = (f32[256,8]{0,1:T(8,128)S(1)}, f32[256,8]{0,1:T(8,128)}, u32[]{:S(2)}) copy-start(f32[256,8]{0,1:T(8,128)} %param.28) | copy-start | bytes 24580
  223.0 18.6 %all-to-all-start.2 = ((bf16[4,2,65536]{2,1,0:T(2,128)(2,1)}), bf16[4,2,65536]{2,1,0:T(2,128)(2,1)S(1)}, u32[]{:S(2)}, u32[]{:S(2)}) async-start(bf16[4,2,65536]{2,1,0:T(2,128)(2,1)} %reshape.299), calls=%async_computation.2 | async-start | bytes 2097152 | tf_op jit(solution)/shard_map/all_to_all | solution.py:125
Sparse Core Ops, SparseCore 0:
  14.7 70.6 all-gather.1
where the time goes:
time: 265 us; the launch traced here: 264 us
  waiting for transfers between devices  65.3 us (25%)
  other arithmetic  61.5 us (23%)
  local copies, waits for them, and re-layouts  54.8 us (21%)
  blocking collectives  42.5 us (16%)
  matrix products  22.3 us (8%)
  between operations  13.8 us (5%)
  starting transfers between devices  3.52 us (1%)
    all_gather x1, waiting for transfers between devices, per_device(): shard_rows = lax.all_gather(attended, ('ep', 'tp'), axis=0, tiled=True)  50.4 us
    unnamed x2, other arithmetic  31.8 us
    all_to_all x1, blocking collectives, per_device(): lax.all_to_all(outgoing_rows, 'ep', split_axis=0, concat_axis=1, tiled=True)  21.7 us
    all_to_all x1, blocking collectives, per_device(): lax.all_to_all(partial_value.astype(jnp.bfloat16), 'ep', split_axis=2, co...  20.9 us
    another operation x3, other arithmetic  18.5 us
    all_to_all x1, waiting for transfers between devices, per_device(): lax.all_to_all(lax.all_to_all(partial_value.astype(jnp.bfloat16), 'ep', s...  14.8 us
    scatter x1, local copies, waits for them, and re-layouts, per_device(): outgoing_rows = jnp.zeros((experts_all * CAP, column_count), jnp.bfloat16...  12.9 us
    unnamed x22, local copies, waits for them, and re-layouts  11.4 us
  transfers between devices with their start and end apart: 2, of which 2 were waited for; matrix products, arithmetic and copies ran while one was open for 8% of the time, Pallas kernels for 0%

commit v1 on v0

v1 whole, which is shorter than its diff:
```python
import functools
import jax
import jax.numpy as jnp
from jax import lax
from jax.sharding import PartitionSpec as P
from jax.experimental import pallas as pl
from jax.experimental.pallas import tpu as pltpu

TOPK = 8
CAP = 64
EPSILON = 1e-06
MESH = pl.DeviceIdType.MESH
BF = jnp.bfloat16
F32 = jnp.float32


def mm(a, b, dims=((1,), (0,))):
    return lax.dot_general(a, b, (dims, ((), ())), preferred_element_type=F32)


def kernel(
    len_ref, pol_ref, ret_ref,
    q_ref, nk_ref, nv_ref, routes_ref, logit_ref, gain_ref,
    k_hbm, v_hbm, ow_hbm, res_hbm, gate_hbm, up_hbm, down_hbm,
    out_ref,
    kbuf, vbuf, pbuf, tbuf, obuf, att, attg, owb, part, recb, resb,
    hid, hg, gu, dn, ptb, psel, wcol, acc, aact,
    psib, pown, srec, qbuf, r1, tb, r2, pk, pkb, xr,
    ksem, vsem, wsem,
    sa, ra, sas, ras, sb, rb, sx, rx, sc, rc, scs, rcs, sds, rds, sd1, rd1, sd2, rd2, sf, rf,
):
    ep = lax.axis_index("ep")
    x = lax.axis_index("tp")
    c = ep % 2
    yz = ep // 2
    y = yz // 4
    z = yz % 4
    sib = (ep + 1 - 2 * c, x)

    def plane_peer(dy, dz):
        return (((y + dy) % 4 * 4 + (z + dz) % 4) * 2 + c, x)

    def x_peer(d):
        return (ep, (x + d) % 4)

    def remote(src, dst, ss, rs, dev):
        return pltpu.make_async_remote_copy(
            src_ref=src, dst_ref=dst, send_sem=ss, recv_sem=rs, device_id=dev, device_id_type=MESH
        )

    bar = pltpu.get_barrier_semaphore()

    for r in range(8):
        pltpu.make_async_copy(k_hbm.at[r], kbuf.at[r], ksem.at[r]).start()
    for r in range(8):
        pltpu.make_async_copy(v_hbm.at[r], vbuf.at[r], vsem.at[r]).start()

    def greet(d, _):
        pl.semaphore_signal(bar, inc=1, device_id=plane_peer(d // 4, d % 4), device_id_type=MESH)
        return 0

    lax.fori_loop(1, 16, greet, 0)
    pl.semaphore_signal(bar, inc=1, device_id=sib, device_id_type=MESH)
    for d in range(1, 4):
        pl.semaphore_signal(bar, inc=1, device_id=x_peer(d), device_id_type=MESH)

    weights = [
        pltpu.make_async_copy(ow_hbm.at[pl.ds(8 * x, 8), 0], owb.at[:, :, pl.ds(0, 128)], wsem.at[0]),
        pltpu.make_async_copy(ow_hbm.at[pl.ds(8 * x, 8), 1], owb.at[:, :, pl.ds(128, 128)], wsem.at[1]),
        pltpu.make_async_copy(res_hbm.at[pl.ds(64 * x, 64)], resb, wsem.at[2]),
        pltpu.make_async_copy(gate_hbm.at[0], gu.at[0, :, pl.ds(0, 384)], wsem.at[3]),
        pltpu.make_async_copy(up_hbm.at[0], gu.at[0, :, pl.ds(384, 384)], wsem.at[4]),
        pltpu.make_async_copy(gate_hbm.at[1], gu.at[1, :, pl.ds(0, 384)], wsem.at[5]),
        pltpu.make_async_copy(up_hbm.at[1], gu.at[1, :, pl.ds(384, 384)], wsem.at[6]),
        pltpu.make_async_copy(down_hbm, dn, wsem.at[7]),
    ]

    scale = 128 ** (-0.5)
    pos = lax.broadcasted_iota(jnp.int32, (1, 1024), 1)
    blk = pos >> 6
    for r in range(8):
        length = len_ref[r]
        pol = pol_ref[r]
        used = (length + 63) >> 6
        low = jnp.where(pol == 0, used - 2, jnp.where(pol == 2, 0, used - 1))
        keep = blk >= low
        for k in range(4):
            named = jnp.where(pol == 1, ret_ref[4 * r + k], -1)
            keep = keep | (blk == named)
        bias = jnp.where(keep & (pos < length), 0.0, -jnp.inf).astype(F32)
        qr = q_ref[r]
        own = jnp.sum(qr.astype(F32) * nk_ref[pl.ds(r, 1), :].astype(F32), axis=1, keepdims=True) * scale
        pltpu.make_async_copy(k_hbm.at[r], kbuf.at[r], ksem.at[r]).wait()
        s = mm(qr, kbuf[r], ((1,), (1,))) * scale + bias
        top = jnp.maximum(jnp.max(s, axis=1, keepdims=True), own)
        p = jnp.exp(s - top)
        ownw = jnp.exp(own - top)
        pbuf[r] = p.astype(BF)
        tbuf[r] = jnp.broadcast_to(jnp.sum(p, axis=1, keepdims=True) + ownw, (16, 128))
        obuf[r] = jnp.broadcast_to(ownw, (16, 128)).astype(BF)
    for w in weights[:3]:
        w.start()
    for r in range(8):
        pltpu.make_async_copy(v_hbm.at[r], vbuf.at[r], vsem.at[r]).wait()
        o = mm(pbuf[r], vbuf[r])
        o = o + obuf[r].astype(F32) * nv_ref[pl.ds(r, 1), :].astype(F32)
        att[pl.ds(16 * r, 16), :] = (o / tbuf[r]).astype(BF)
    for w in weights[3:]:
        w.start()
    rows = lax.broadcasted_iota(jnp.int32, (128, 128), 0)
    cols = lax.broadcasted_iota(jnp.int32, (128, 128), 1)
    perm = jnp.where(cols == (rows % 8) * 16 + rows // 8, 1.0, 0.0).astype(BF)
    attg[yz, c] = mm(perm, att[...]).astype(BF)

    pl.semaphore_wait(bar, 19)

    def send_a(d, _):
        remote(attg.at[yz, c], attg.at[yz, c], sa.at[d], ra.at[d], plane_peer(d // 4, d % 4)).start()
        return 0

    lax.fori_loop(1, 16, send_a, 0)
    remote(attg.at[yz, c], attg.at[yz, c], sas.at[0], ras.at[0], sib).start()

    routes = routes_ref[...]
    logits = logit_ref[...]
    grown = jnp.exp(logits - jnp.max(logits, axis=1, keepdims=True))
    rw = grown / jnp.sum(grown, axis=1, keepdims=True)
    lane = lax.broadcasted_iota(jnp.int32, (256, 128), 1)
    mems, ws = [], []
    for e in range(2):
        hit = routes == ep * 2 + e
        mems.append(jnp.sum(jnp.where(hit, 1.0, 0.0), axis=1, keepdims=True))
        ws.append(jnp.sum(jnp.where(hit, rw, 0.0), axis=1, keepdims=True))
    memb = jnp.where(lane < 64, mems[0], mems[1])
    tri = jnp.where(
        lax.broadcasted_iota(jnp.int32, (256, 256), 1) < lax.broadcasted_iota(jnp.int32, (256, 256), 0), 1.0, 0.0
    ).astype(BF)
    rank = mm(tri, memb.astype(BF))
    slot = jnp.where(lane < 64, lane, lane - 64).astype(F32)
    pt = jnp.where(rank == slot, memb, 0.0)
    psel[...] = pt.T.astype(BF)
    for e in range(2):
        inside = (lane < 64) if e == 0 else (lane >= 64)
        ptb[e] = jnp.where(inside, pt, 0.0).astype(BF)
        wcol[e] = jnp.broadcast_to(ws[e], (256, 128))

    def pass_a(d, _):
        src = (y + 4 - d // 4) % 4 * 4 + (z + 4 - d % 4) % 4
        remote(attg.at[src, c], attg.at[src, c], sa.at[d], ra.at[d], sib).wait_recv()
        remote(attg.at[src, c], attg.at[src, c], sas.at[d], ras.at[d], sib).start()
        return 0

    lax.fori_loop(1, 16, pass_a, 0)

    weights[0].wait()
    weights[1].wait()

    def project(cc):
        total = jnp.zeros((256, 256), F32)
        for g in range(8):
            lhs = attg[:, cc, pl.ds(16 * g, 16), :].reshape(256, 128)
            total = total + mm(lhs, owb[g])
        total = total.reshape(16, 16, 256)
        part[:, cc] = total[:, :8, :128] + total[:, 8:, 128:]

    project(c)

    def got_a(d, _):
        src = (y + 4 - d // 4) % 4 * 4 + (z + 4 - d % 4) % 4
        remote(attg.at[src, 1 - c], attg.at[src, 1 - c], sas.at[d], ras.at[d], sib).wait_recv()
        return 0

    lax.fori_loop(0, 16, got_a, 0)
    project(1 - c)

    for d in range(1, 4):
        to = (x + d) % 4
        remote(part.at[pl.ds(4 * to, 4)], recb.at[d], sb.at[d], rb.at[d], x_peer(d)).start()
    weights[2].wait()
    total = part[pl.ds(4 * x, 4)].reshape(64, 128)
    for d in range(1, 4):
        remote(recb.at[d], recb.at[d], sb.at[d], rb.at[d], x_peer(d)).wait_recv()
        total = total + recb[d].reshape(64, 128)
    mine = pl.ds(pl.multiple_of(64 * x, 64), 64)
    hid[yz, c, mine, :] = (resb[...].astype(F32) + total).astype(BF)

    for d in range(1, 4):
        remote(hid.at[yz, c, mine], hid.at[yz, c, mine], sx.at[d], rx.at[d], x_peer(d)).start()
    for d in range(1, 4):
        there = pl.ds(pl.multiple_of(64 * ((x + 4 - d) % 4), 64), 64)
        remote(hid.at[yz, c, there], hid.at[yz, c, there], sx.at[d], rx.at[d], x_peer(d)).wait_recv()

    def first_axis(d):
        return plane_peer(d * c, d * (1 - c))

    def second_axis(d):
        return plane_peer(d * (1 - c), d * c)

    def origin(d1, d2):
        dy = d1 * c + d2 * (1 - c)
        dz = d1 * (1 - c) + d2 * c
        return (y + 4 - dy) % 4 * 4 + (z + 4 - dz) % 4, dy * 4 + dz

    def copy_c(src, d1, d2, dev):
        return remote(hid.at[src, c], hid.at[src, c], sc.at[4 * d1 + d2], rc.at[4 * d1 + d2], dev)

    def got_plane(d1, d2):
        copy_c(origin(d1, d2)[0], d1, d2, sib).wait_recv()

    def copy_cs(d1, d2):
        src, at = origin(d1, d2)
        return remote(hid.at[src, c], hid.at[src, c], scs.at[at], rcs.at[at], sib)

    for d in range(1, 4):
        copy_c(yz, d, 0, first_axis(d)).start()
    for d1 in range(4):
        if d1:
            got_plane(d1, 0)
        for d2 in range(1, 4):
            copy_c(origin(d1, 0)[0], d1, d2, second_axis(d2)).start()
        copy_cs(d1, 0).start()

    lane64 = lax.broadcasted_iota(jnp.int32, (64, 128), 1) // 32

    def pack(value, j):
        out = jnp.zeros((64, 128), F32)
        for k in range(4):
            piece = value[64 * k : 64 * k + 64]
            shift = (32 * (k - j)) % 128
            if shift:
                piece = pltpu.roll(piece, shift, 1)
            out = jnp.where(lane64 == k, piece, out)
        return out

    block = hid[yz, c].astype(F32)
    for j in range(4):
        pk[j] = pack(block, j)
    base = pk[x]

    def pass_c(n, _):
        d1, d2 = n % 4, n // 4
        got_plane(d1, d2)
        copy_cs(d1, d2).start()
        return 0

    lax.fori_loop(4, 16, pass_c, 0)

    def got_c(at, _):
        src = (y + 4 - at // 4) % 4 * 4 + (z + 4 - at % 4) % 4
        remote(hid.at[src, 1 - c], hid.at[src, 1 - c], scs.at[at], rcs.at[at], sib).wait_recv()
        return 0

    lax.fori_loop(0, 16, got_c, 0)

    def pick(b, squares):
        for h in range(2):
            rows_of = mm(psel[...], hid[b, h])
            squares = squares + rows_of * rows_of
            at = pl.multiple_of((2 * b + h) * 128, 128)
            hg[:, pl.ds(at, 128)] = (rows_of * gain_ref[pl.ds(2 * b + h, 1), :]).astype(BF)
        return squares

    squares = lax.fori_loop(0, 16, pick, jnp.zeros((128, 128), F32))
    rs = lax.rsqrt(jnp.sum(squares, axis=1, keepdims=True) / 4096 + EPSILON)
    for w in weights[3:]:
        w.wait()
    for e in range(2):
        for n in range(3):
            acc[e, :, pl.ds(256 * n, 256)] = mm(hg[pl.ds(64 * e, 64), :], gu[e, :, pl.ds(256 * n, 256)])
    halves = []
    for e in range(2):
        re = rs[64 * e : 64 * e + 64]
        gate = acc[e, :, pl.ds(0, 384)] * re
        up = acc[e, :, pl.ds(384, 384)] * re
        halves.append((gate / (1.0 + jnp.exp(-gate)) * up).astype(BF))
    act = jnp.concatenate(halves, axis=0)
    for e in range(2):
        spread = mm(ptb[e], act)
        aact[:, pl.ds(384 * e, 384)] = (spread * wcol[e][:, :1]).astype(BF)

    def dest(n, cc):
        i1 = n // 4
        d1 = jnp.where(i1 == 0, 2, jnp.where(i1 == 1, 1, jnp.where(i1 == 2, 3, 0)))
        d2 = n % 4
        dy = d1 * (1 - cc) + d2 * cc
        dz = d2 * (1 - cc) + d1 * cc
        return d1, d2, (y + dy) % 4 * 4 + (z + dz) % 4

    def down(n):
        _, _, mine_at = dest(n, c)
        _, _, sib_at = dest(n, 1 - c)
        mine_col = pl.multiple_of((2 * mine_at + c) * 128, 128)
        sib_col = pl.multiple_of((2 * sib_at + 1 - c) * 128, 128)
        rhs = jnp.concatenate([dn[:, pl.ds(sib_col, 128)], dn[:, pl.ds(mine_col, 128)]], axis=1)
        got = mm(aact[...], rhs)
        psib[n] = got[:, :128].astype(BF)
        pown[n] = got[:, 128:]
        remote(psib.at[n], srec.at[n], sds.at[n], rds.at[n], sib).start()

    def join(n):
        remote(psib.at[n], srec.at[n], sds.at[n], rds.at[n], sib).wait_recv()
        return pown[n] + srec[n].astype(F32)

    def copy_d1(n):
        d1, d2, _ = dest(n, c)
        dev = plane_peer(d1 * (1 - c), d1 * c)
        return remote(qbuf.at[n], r1.at[n], sd1.at[n], rd1.at[n], dev)

    def forward(n):
        qbuf[n] = join(n).astype(BF)
        copy_d1(n).start()

    down(0)

    def step(n, _):
        down(n)
        forward(n - 1)
        return 0

    lax.fori_loop(1, 13, step, 0)
    for n in range(13, 16):
        down(n)

    def copy_d2(d2):
        return remote(tb.at[d2], r2.at[d2], sd2.at[d2], rd2.at[d2], plane_peer(d2 * c, d2 * (1 - c)))

    for d2 in (2, 1, 3, 0):
        total = join(12 + d2)
        for i1 in range(3):
            n = 4 * i1 + d2
            copy_d1(n).wait_recv()
            total = total + r1[n].astype(F32)
        if d2:
            tb[d2] = total.astype(BF)
            copy_d2(d2).start()
    for d2 in (1, 3, 2):
        copy_d2(d2).wait_recv()
        total = total + r2[d2].astype(F32)

    for j in range(4):
        packed = pack(total, j)
        pk[j] = packed
        pkb[j] = packed.astype(BF)
    copies = []
    for d in (2, 1, 3):
        cp = remote(pkb.at[(x + d) % 4], xr.at[d], sf.at[d], rf.at[d], x_peer(d))
        cp.start()
        copies.append(cp)
    total = pk[x]
    for d in (1, 3, 2):
        remote(xr.at[d], xr.at[d], sf.at[d], rf.at[d], x_peer(d)).wait_recv()
        total = total + xr[d].astype(F32)
    total = (base + total).astype(BF)
    for k in range(4):
        out_ref[pl.ds(64 * k, 64), :] = total[:, 32 * k : 32 * k + 32]

    def drain_plane(d, _):
        remote(attg.at[yz, c], attg.at[yz, c], sa.at[d], ra.at[d], sib).wait_send()
        copy_c(yz, d // 4, d % 4, sib).wait_send()
        return 0

    def drain_sib(d, _):
        remote(attg.at[yz, c], attg.at[yz, c], sas.at[d], ras.at[d], sib).wait_send()
        remote(hid.at[yz, c], hid.at[yz, c], scs.at[d], rcs.at[d], sib).wait_send()
        remote(psib.at[d], srec.at[d], sds.at[d], rds.at[d], sib).wait_send()
        return 0

    def drain_d1(n, _):
        copy_d1(n).wait_send()
        return 0

    lax.fori_loop(1, 16, drain_plane, 0)
    lax.fori_loop(0, 16, drain_sib, 0)
    lax.fori_loop(0, 12, drain_d1, 0)
    for d in range(1, 4):
        remote(part.at[pl.ds(4 * ((x + d) % 4), 4)], recb.at[d], sb.at[d], rb.at[d], x_peer(d)).wait_send()
        remote(hid.at[yz, c, mine], hid.at[yz, c, mine], sx.at[d], rx.at[d], x_peer(d)).wait_send()
        copy_d2(d).wait_send()
    for cp in copies:
        cp.wait_send()


def per_device(
    queries, key_cache, stored_value_cache, new_key, incoming_value, lengths, policy, retained_blocks,
    out_weight, residual, norm_gain, routes, router_logits, gate_weight, up_weight, down_weight,
):
    vm = pl.BlockSpec(memory_space=pltpu.VMEM)
    sm = pl.BlockSpec(memory_space=pltpu.SMEM)
    hb = pl.BlockSpec(memory_space=pl.ANY)
    dma = pltpu.SemaphoreType.DMA
    scratch = [
        pltpu.VMEM((8, 1024, 128), BF),
        pltpu.VMEM((8, 1024, 128), BF),
        pltpu.VMEM((8, 16, 1024), BF),
        pltpu.VMEM((8, 16, 128), F32),
        pltpu.VMEM((8, 16, 128), BF),
        pltpu.VMEM((128, 128), BF),
        pltpu.VMEM((16, 2, 128, 128), BF),
        pltpu.VMEM((8, 128, 256), BF),
        pltpu.VMEM((16, 2, 8, 128), F32),
        pltpu.VMEM((4, 4, 2, 8, 128), F32),
        pltpu.VMEM((64, 128), BF),
        pltpu.VMEM((16, 2, 256, 128), BF),
        pltpu.VMEM((128, 4096), BF),
        pltpu.VMEM((2, 4096, 768), BF),
        pltpu.VMEM((768, 4096), BF),
        pltpu.VMEM((2, 256, 128), BF),
        pltpu.VMEM((128, 256), BF),
        pltpu.VMEM((2, 256, 128), F32),
        pltpu.VMEM((2, 64, 768), F32),
        pltpu.VMEM((256, 768), BF),
        pltpu.VMEM((16, 256, 128), BF),
        pltpu.VMEM((16, 256, 128), F32),
        pltpu.VMEM((16, 256, 128), BF),
        pltpu.VMEM((12, 256, 128), BF),
        pltpu.VMEM((12, 256, 128), BF),
        pltpu.VMEM((4, 256, 128), BF),
        pltpu.VMEM((4, 256, 128), BF),
        pltpu.VMEM((4, 64, 128), F32),
        pltpu.VMEM((4, 64, 128), BF),
        pltpu.VMEM((4, 64, 128), BF),
        dma((8,)), dma((8,)), dma((8,)),
        dma((16,)), dma((16,)), dma((16,)), dma((16,)),
        dma((4,)), dma((4,)), dma((4,)), dma((4,)),
        dma((16,)), dma((16,)), dma((16,)), dma((16,)),
        dma((16,)), dma((16,)), dma((12,)), dma((12,)),
        dma((4,)), dma((4,)), dma((4,)), dma((4,)),
    ]
    return pl.pallas_call(
        kernel,
        out_shape=jax.ShapeDtypeStruct((256, 32), BF),
        in_specs=[sm] * 3 + [vm] * 6 + [hb] * 7,
        out_specs=vm,
        scratch_shapes=scratch,
        name="decode_step",
        cost_estimate=pl.CostEstimate(flops=3_000_000_000, bytes_accessed=26_000_000, transcendentals=200_000),
        compiler_params=pltpu.CompilerParams(
            collective_id=0, has_side_effects=True, vmem_limit_bytes=56 * 2**20
        ),
    )(
        lengths, policy.reshape(8), retained_blocks.reshape(32),
        queries, new_key.reshape(8, 128), incoming_value.reshape(8, 128),
        routes, router_logits, norm_gain.reshape(32, 128),
        key_cache.reshape(8, 1024, 128), stored_value_cache.reshape(8, 1024, 128),
        out_weight.reshape(32, 2, 128, 128), residual,
        gate_weight, up_weight, down_weight.reshape(768, 4096),
    )


def solution(mesh):
    return jax.shard_map(
        per_device,
        mesh=mesh,
        in_specs=(
            P("ep", "tp", None),
            P("ep", "tp", None, None),
            P("ep", "tp", None, None),
            P("ep", "tp", None),
            P("ep", "tp", None),
            P("ep"),
            P("ep", "tp"),
            P("ep", "tp", None),
            P(None, "ep"),
            P(None, "ep"),
            P(),
            P(),
            P(),
            P("ep", None, "tp"),
            P("ep", None, "tp"),
            P("ep", "tp", None),
        ),
        out_specs=P(None, ("ep", "tp")),
        check_vma=False,
    )
```

time: 265 us -> 78.1 us (0.29)
  the two profiles are of different devices: /device:TPU:1 before, /device:TPU:8 now
where the time goes in v1:
time: 78.1 us; the launch traced here: 77.8 us
  Pallas kernels  72 us (92%)
  local copies, waits for them, and re-layouts  5.82 us (7%)
    pallas_call x1, Pallas kernels, per_device(): pl.pallas_call(kernel, out_shape=jax.ShapeDtypeStruct((256, 32), BF), in_...  72 us
    unnamed x3, local copies, waits for them, and re-layouts  3.7 us

profile of v1, /device:TPU:8, one launch (start us, length us, event | category | flops | bytes accessed | tf_op | source)
XLA Modules:
  0.0 77.8 jit_solution(7093098807885339039)
XLA Ops:
  0.0 0.8 copy.21
  0.8 0.6 reshape.28.ret_ref
  1.4 1.5 %copy.22.routes_ref = s32[256,8]{1,0:T(8,128)} copy(s32[256,8]{0,1:T(8,128)} %param.27) | data formatting | bytes 16384 | tf_op args[11]
  2.8 1.5 %copy.23.logit_ref = f32[256,8]{1,0:T(8,128)} copy(f32[256,8]{0,1:T(8,128)} %param.28) | data formatting | bytes 16384 | tf_op args[12]
  4.3 72.0 %decode_step.1 = bf16[256,32]{1,0:T(8,128)(2,1)} custom-call(s32[8]{0:T(128)} %len_ref.1, s32[8]{0:T(128)} %bitcast.17, s32[32]{0:T(128)} %reshape.28.ret_ref, bf16[8,16,128]{2,1,0:T(8,128)(2,1)} %q_ref.1, bf16[8,128]{1,0:T(8,128)(2,1)} %bitcast.15, bf16[8,128]{1,0:T(8,128)(2,1)} %bitcast.16, s32[256,8]{1,0:T(8,128)} %copy.22.routes_ref, ...), custom_call_target="tpu_custom_call" | custom-call | flops 3000000000 | bytes 26000000 | tf_op jit(solution)/shard_map/decode_step/pallas_call | solution.py:429
  76.3 1.5 %copy.24 = bf16[256,32]{0,1:T(8,128)(2,1)} copy(bf16[256,32]{1,0:T(8,128)(2,1)} %decode_step.1) | data formatting | bytes 32768 | tf_op jit(solution)/shard_map/decode_step/pallas_call | solution.py:429

commit v2 on v1

v2 whole, which is shorter than its diff:
```python
import functools
import jax
import jax.numpy as jnp
from jax import lax
from jax.sharding import PartitionSpec as P
from jax.experimental import pallas as pl
from jax.experimental.pallas import tpu as pltpu

TOPK = 8
CAP = 64
EPSILON = 1e-06
MESH = pl.DeviceIdType.MESH
BF = jnp.bfloat16
F32 = jnp.float32


def mm(a, b, dims=((1,), (0,))):
    return lax.dot_general(a, b, (dims, ((), ())), preferred_element_type=F32)


def kernel(
    len_hbm, pol_hbm, ret_hbm, q_hbm, nk_hbm, nv_hbm, routes_hbm, logit_hbm, gain_hbm,
    k_hbm, v_hbm, ow_hbm, res_hbm, gate_hbm, up_hbm, down_hbm,
    out_ref,
    len_ref, pol_ref, ret_ref, q_ref, nk_ref, nv_ref, routes_ref, logit_ref, gain_ref,
    kbuf, vbuf, pbuf, tbuf, obuf, att, attg, owb, pb, nat, resb,
    hid, sq, gu, dn, ptb, psel, wcol, acc, aact,
    psib, pown, srec, qbuf, r1, tb, last, block, r2,
    small, ksem, vsem, wsem,
    sa, ra, sas, ras, sb, rb, sc, rc, scs, rcs, sds, rds, sd1, rd1, sd2, rd2,
):
    ep = lax.axis_index("ep")
    x = lax.axis_index("tp")
    c = ep % 2
    yz = ep // 2
    y = yz // 4
    z = yz % 4
    a1 = z * (1 - c) + y * c
    a2 = y * (1 - c) + z * c
    sib = (ep + 1 - 2 * c, x)
    near = (1, 3, 2)

    def peer(dx, dy, dz):
        return (((y + dy) % 4 * 4 + (z + dz) % 4) * 2 + c, (x + dx) % 4)

    def over_axis1(d):
        return peer(0, d * c, d * (1 - c))

    def over_axis2(d, dx=0):
        return peer(dx, d * (1 - c), d * c)

    def remote(src, dst, ss, rs, dev):
        return pltpu.make_async_remote_copy(
            src_ref=src, dst_ref=dst, send_sem=ss, recv_sem=rs, device_id=dev, device_id_type=MESH
        )

    def sent(ref, sem):
        remote(ref, ref, sem, rb.at[0], sib).wait_send()

    def got(ref, sem):
        remote(ref, ref, sb.at[0], sem, sib).wait_recv()

    bar = pltpu.get_barrier_semaphore()
    partners = [sib] + [peer(d, 0, 0) for d in near] + [peer(0, d, 0) for d in near] + [peer(0, 0, d) for d in near]
    for dev in partners:
        pl.semaphore_signal(bar, inc=1, device_id=dev, device_id_type=MESH)

    smalls = [
        pltpu.make_async_copy(src, dst, small.at[i])
        for i, (src, dst) in enumerate((
            (routes_hbm, routes_ref), (logit_hbm, logit_ref),
            (len_hbm, len_ref), (pol_hbm, pol_ref), (ret_hbm, ret_ref),
            (q_hbm, q_ref), (nk_hbm, nk_ref), (nv_hbm, nv_ref), (gain_hbm, gain_ref),
        ))
    ]
    for cp in smalls:
        cp.start()
    for r in range(8):
        pltpu.make_async_copy(k_hbm.at[r], kbuf.at[r], ksem.at[r]).start()
    for r in range(8):
        pltpu.make_async_copy(v_hbm.at[r], vbuf.at[r], vsem.at[r]).start()
    weights = [
        pltpu.make_async_copy(ow_hbm.at[pl.ds(8 * x, 8), 0], owb.at[:, :, pl.ds(0, 128)], wsem.at[0]),
        pltpu.make_async_copy(ow_hbm.at[pl.ds(8 * x, 8), 1], owb.at[:, :, pl.ds(128, 128)], wsem.at[1]),
        pltpu.make_async_copy(res_hbm, resb, wsem.at[2]),
        pltpu.make_async_copy(gate_hbm.at[0], gu.at[0, :, pl.ds(0, 384)], wsem.at[3]),
        pltpu.make_async_copy(up_hbm.at[0], gu.at[0, :, pl.ds(384, 384)], wsem.at[4]),
        pltpu.make_async_copy(gate_hbm.at[1], gu.at[1, :, pl.ds(0, 384)], wsem.at[5]),
        pltpu.make_async_copy(up_hbm.at[1], gu.at[1, :, pl.ds(384, 384)], wsem.at[6]),
        pltpu.make_async_copy(down_hbm, dn, wsem.at[7]),
    ]

    for cp in smalls:
        cp.wait()

    logits = logit_ref[...]
    grown = jnp.exp(logits - jnp.max(logits, axis=0, keepdims=True))
    rw = grown / jnp.sum(grown, axis=0, keepdims=True)
    sub = lax.broadcasted_iota(jnp.int32, (128, 256), 0)
    mem, wrow = [], []
    for e in range(2):
        hit = routes_ref[...] == ep * 2 + e
        mem.append(jnp.sum(jnp.where(hit, 1.0, 0.0), axis=0, keepdims=True))
        wrow.append(jnp.sum(jnp.where(hit, rw, 0.0), axis=0, keepdims=True))
    memb = jnp.where(sub < 64, mem[0], mem[1])
    tri = jnp.where(
        lax.broadcasted_iota(jnp.int32, (256, 256), 0) < lax.broadcasted_iota(jnp.int32, (256, 256), 1), 1.0, 0.0
    ).astype(BF)
    rank = mm(memb.astype(BF), tri)
    slot = jnp.where(sub < 64, sub, sub - 64).astype(F32)
    chosen = jnp.where(rank == slot, memb, 0.0)
    psel[...] = chosen.astype(BF)
    spread_t = chosen.T
    weight_t = (chosen * jnp.where(sub < 64, wrow[0], wrow[1])).T
    lane = lax.broadcasted_iota(jnp.int32, (256, 128), 1)
    for e in range(2):
        inside = (lane < 64) if e == 0 else (lane >= 64)
        ptb[e] = jnp.where(inside, spread_t, 0.0).astype(BF)
        wcol[e] = jnp.broadcast_to(jnp.sum(jnp.where(inside, weight_t, 0.0), axis=1, keepdims=True), (256, 128))

    scale = 128 ** (-0.5)
    pos = lax.broadcasted_iota(jnp.int32, (1, 1024), 1)
    blk = pos >> 6
    for r in range(8):
        length = len_ref[r]
        pol = pol_ref[r]
        used = (length + 63) >> 6
        low = jnp.where(pol == 0, used - 2, jnp.where(pol == 2, 0, used - 1))
        keep = blk >= low
        for k in range(4):
            named = jnp.where(pol == 1, ret_ref[k, r], -1)
            keep = keep | (blk == named)
        bias = jnp.where(keep & (pos < length), 0.0, -jnp.inf).astype(F32)
        qr = q_ref[r]
        own = jnp.sum(qr.astype(F32) * nk_ref[pl.ds(r, 1), :].astype(F32), axis=1, keepdims=True) * scale
        pltpu.make_async_copy(k_hbm.at[r], kbuf.at[r], ksem.at[r]).wait()
        s = mm(qr, kbuf[r], ((1,), (1,))) * scale + bias
        top = jnp.maximum(jnp.max(s, axis=1, keepdims=True), own)
        p = jnp.exp(s - top)
        ownw = jnp.exp(own - top)
        pbuf[r] = p.astype(BF)
        tbuf[r] = jnp.broadcast_to(jnp.sum(p, axis=1, keepdims=True) + ownw, (16, 128))
        obuf[r] = jnp.broadcast_to(ownw, (16, 128)).astype(BF)
    for w in weights[:3]:
        w.start()
    for r in range(8):
        pltpu.make_async_copy(v_hbm.at[r], vbuf.at[r], vsem.at[r]).wait()
        o = mm(pbuf[r], vbuf[r])
        o = o + obuf[r].astype(F32) * nv_ref[pl.ds(r, 1), :].astype(F32)
        att[pl.ds(16 * r, 16), :] = (o / tbuf[r]).astype(BF)
    for w in weights[3:]:
        w.start()
    rows = lax.broadcasted_iota(jnp.int32, (128, 128), 0)
    cols = lax.broadcasted_iota(jnp.int32, (128, 128), 1)
    perm = jnp.where(cols == (rows % 8) * 16 + rows // 8, 1.0, 0.0).astype(BF)
    here = 4 * a2 + a1
    attg[c, here] = mm(perm, att[...]).astype(BF)

    pl.semaphore_wait(bar, len(partners))

    class Gather:
        def __init__(self, buf, sends, gets, sib_sends, sib_gets):
            self.buf, self.sends, self.gets = buf, sends, gets
            self.sib_sends, self.sib_gets = sib_sends, sib_gets

        def row(self, d2, cc):
            base = a2 if cc is c else a1
            return self.buf.at[cc, pl.ds(4 * ((base + 4 - d2) % 4), 4)]

        def send(self, d1, get, dev):
            at = self.buf.at[c, 4 * a2 + (a1 + 4 - d1) % 4]
            remote(at, at, self.sends.at[0], self.gets.at[get], dev).start()

        def over(self, d2):
            at = self.row(d2, c)
            remote(at, at, self.sib_sends.at[0], self.sib_gets.at[d2], sib).start()

        def start(self):
            for d in near:
                self.send(0, 4 + d, over_axis1(d))
            for d in near:
                self.send(0, d, over_axis2(d))

        def relay(self):
            for d1 in near:
                got(self.buf.at[c, 4 * a2 + (a1 + 4 - d1) % 4], self.gets.at[4 + d1])
                for d2 in near:
                    self.send(d1, d2, over_axis2(d2))
            self.over(0)

        def pass_on(self, d2):
            got(self.row(d2, c), self.gets.at[d2])
            self.over(d2)

        def arrived(self, d2):
            got(self.row(d2, 1 - c), self.sib_gets.at[d2])

        def finish(self):
            sent(self.buf.at[c, pl.ds(0, 15)], self.sends.at[0])
            sent(self.buf.at[c], self.sib_sends.at[0])

    attended = Gather(attg, sa, ra, sas, ras)
    attended.start()
    attended.relay()
    for d in near:
        attended.pass_on(d)

    weights[0].wait()
    weights[1].wait()

    def project(cc, half):
        total = jnp.zeros((256, 256), F32)
        for g in range(8):
            lhs = attg[cc, :, pl.ds(16 * g, 16), :].reshape(256, 128)
            total = total + mm(lhs, owb[g])
        total = total.reshape(16, 16, 256)
        total = total[:, :8, :128] + total[:, 8:, 128:]
        pb[x, cc] = total.reshape(128, 128).astype(BF)
        for d in near:
            remote(pb.at[x, cc], pb.at[x, cc], sb.at[0], rb.at[2 * d + half], peer(d, 0, 0)).start()

    project(c, 0)
    for d in (0,) + near:
        attended.arrived(d)
    project(1 - c, 1)
    attended.finish()
    weights[2].wait()
    for half, cc in ((0, c), (1, 1 - c)):
        for d in near:
            got(pb.at[(x + 4 - d) % 4, cc], rb.at[2 * d + half])
    for cc in range(2):
        total = pb[0, cc].astype(F32)
        for j in range(1, 4):
            total = total + pb[j, cc].astype(F32)
        total = total.reshape(16, 8, 128)
        for at in range(16):
            nat[at if cc == 0 else at % 4 * 4 + at // 4, cc] = total[at]
    hid[c, here] = (resb[...].astype(F32) + nat[...].reshape(256, 128)).astype(BF)

    hidden = Gather(hid, sc, rc, scs, rcs)
    hidden.start()
    sent(pb.at[pl.ds(0, 3)], sb.at[0])
    block[...] = hid[c, here].astype(F32).T
    hidden.relay()
    for w in weights[3:]:
        w.wait()

    def products(d2, cc, first):
        row = ((a2 if cc is c else a1) + 4 - d2) % 4
        at = [(4 * row + k) * (1 - cc) + (4 * k + row) * cc for k in range(4)]
        picked = mm(psel[...], jnp.concatenate([hid[cc, 4 * row + k] for k in range(4)], axis=1))
        squares = picked * picked
        gain = jnp.concatenate([gain_ref[pl.ds(2 * b + cc, 1), :] for b in at], axis=1)
        squares = squares[:, :128] + squares[:, 128:256] + squares[:, 256:384] + squares[:, 384:]
        lhs = (picked * gain).astype(BF)
        cols = [pl.ds(pl.multiple_of((2 * b + cc) * 128, 128), 128) for b in at]
        for e in range(2):
            rhs = jnp.concatenate([gu[e, col, :] for col in cols], axis=0)
            part = mm(lhs[64 * e : 64 * e + 64], rhs)
            acc[e] = part if first else acc[e] + part
        sq[...] = squares if first else sq[...] + squares

    products(0, c, True)
    waiting = 0
    for d2 in near:
        hidden.pass_on(d2)
        hidden.arrived(waiting)
        products(waiting, 1 - c, False)
        products(d2, c, False)
        waiting = d2
    hidden.arrived(waiting)
    products(waiting, 1 - c, False)
    rs = lax.rsqrt(jnp.sum(sq[...], axis=1, keepdims=True) / 4096 + EPSILON)
    halves = []
    for e in range(2):
        re = rs[64 * e : 64 * e + 64]
        gate = acc[e, :, pl.ds(0, 384)] * re
        up = acc[e, :, pl.ds(384, 384)] * re
        halves.append((gate / (1.0 + jnp.exp(-gate)) * up).astype(BF))
    act = jnp.concatenate(halves, axis=0)
    for e in range(2):
        spread = mm(ptb[e], act)
        aact[:, pl.ds(384 * e, 384)] = (spread * wcol[e][:, :1]).astype(BF)

    def dest(n, cc):
        i1 = n // 4
        d1 = jnp.where(i1 == 0, 2, jnp.where(i1 == 1, 1, jnp.where(i1 == 2, 3, 0)))
        d2 = n % 4
        dy = d1 * (1 - cc) + d2 * cc
        dz = d2 * (1 - cc) + d1 * cc
        return d1, d2, (y + dy) % 4 * 4 + (z + dz) % 4

    def down(n):
        mine_col = pl.multiple_of((2 * dest(n, c)[2] + c) * 128, 128)
        sib_col = pl.multiple_of((2 * dest(n, 1 - c)[2] + 1 - c) * 128, 128)
        rhs = jnp.concatenate([dn[:, pl.ds(sib_col, 128)], dn[:, pl.ds(mine_col, 128)]], axis=1)
        both = mm(aact[...], rhs)
        psib[n] = both[:, :128].astype(BF)
        remote(psib.at[n], srec.at[n], sds.at[0], rds.at[n], sib).start()
        pown[n] = both[:, 128:]

    def join(n):
        got(srec.at[n], rds.at[n])
        return pown[n] + srec[n].astype(F32)

    def forward(n):
        d1, d2, _ = dest(n, c)
        qbuf[n] = join(n).astype(BF)
        to = r1.at[d2, n // 4]
        remote(qbuf.at[n], to, sd1.at[0], rd1.at[d2], peer(0, d1 * (1 - c), d1 * c)).start()

    down(0)

    def step(n, _):
        down(n)
        forward(n - 1)
        return 0

    lax.fori_loop(1, 13, step, 0)
    for n in range(13, 16):
        down(n)
    hidden.finish()

    def slab(j):
        return pl.ds(pl.multiple_of(32 * (j % 4), 32), 32)

    for d2 in (2, 1, 3, 0):
        total = join(12 + d2)
        got(r1.at[d2], rd1.at[d2])
        for i1 in range(3):
            total = total + r1[d2, i1].astype(F32)
        turned = total.T
        tb[d2] = turned.astype(BF)
        if d2 == 0:
            last[...] = block[slab(x), :] + jnp.where(x == 0, turned[:32], jnp.where(x == 1, turned[32:64], jnp.where(x == 2, turned[64:96], turned[96:])))
        for dx in (2, 1, 3, 0):
            if d2 or dx:
                dev = peer(dx, d2 * c, d2 * (1 - c))
                remote(tb.at[d2, slab(x + dx)], r2.at[4 * d2 + dx], sd2.at[0], rd2.at[0], dev).start()
    sent(psib, sds.at[0])
    sent(qbuf, sd1.at[0])
    got(r2.at[pl.ds(1, 15)], rd2.at[0])
    total = last[...]
    for k in range(1, 16):
        total = total + r2[k].astype(F32)
    out_ref[...] = total.astype(BF)
    sent(r2.at[pl.ds(1, 15)], sd2.at[0])


def per_device(
    queries, key_cache, stored_value_cache, new_key, incoming_value, lengths, policy, retained_blocks,
    out_weight, residual, norm_gain, routes, router_logits, gate_weight, up_weight, down_weight,
):
    vm = pl.BlockSpec(memory_space=pltpu.VMEM)
    hb = pl.BlockSpec(memory_space=pl.ANY)
    dma = pltpu.SemaphoreType.DMA
    scratch = [
        pltpu.SMEM((8,), jnp.int32),
        pltpu.SMEM((8,), jnp.int32),
        pltpu.SMEM((4, 8), jnp.int32),
        pltpu.VMEM((8, 16, 128), BF),
        pltpu.VMEM((8, 128), BF),
        pltpu.VMEM((8, 128), BF),
        pltpu.VMEM((8, 256), jnp.int32),
        pltpu.VMEM((8, 256), F32),
        pltpu.VMEM((32, 128), F32),
        pltpu.VMEM((8, 1024, 128), BF),
        pltpu.VMEM((8, 1024, 128), BF),
        pltpu.VMEM((8, 16, 1024), BF),
        pltpu.VMEM((8, 16, 128), F32),
        pltpu.VMEM((8, 16, 128), BF),
        pltpu.VMEM((128, 128), BF),
        pltpu.VMEM((2, 16, 128, 128), BF),
        pltpu.VMEM((8, 128, 256), BF),
        pltpu.VMEM((4, 2, 128, 128), BF),
        pltpu.VMEM((16, 2, 8, 128), F32),
        pltpu.VMEM((256, 128), BF),
        pltpu.VMEM((2, 16, 256, 128), BF),
        pltpu.VMEM((128, 128), F32),
        pltpu.VMEM((2, 4096, 768), BF),
        pltpu.VMEM((768, 4096), BF),
        pltpu.VMEM((2, 256, 128), BF),
        pltpu.VMEM((128, 256), BF),
        pltpu.VMEM((2, 256, 128), F32),
        pltpu.VMEM((2, 64, 768), F32),
        pltpu.VMEM((256, 768), BF),
        pltpu.VMEM((16, 256, 128), BF),
        pltpu.VMEM((16, 256, 128), F32),
        pltpu.VMEM((16, 256, 128), BF),
        pltpu.VMEM((12, 256, 128), BF),
        pltpu.VMEM((4, 3, 256, 128), BF),
        pltpu.VMEM((4, 128, 256), BF),
        pltpu.VMEM((32, 256), F32),
        pltpu.VMEM((128, 256), F32),
        pltpu.VMEM((16, 32, 256), BF),
        dma((9,)), dma((8,)), dma((8,)), dma((8,)),
        dma((1,)), dma((8,)), dma((1,)), dma((4,)),
        dma((1,)), dma((8,)),
        dma((1,)), dma((8,)), dma((1,)), dma((4,)),
        dma((1,)), dma((16,)), dma((1,)), dma((4,)),
        dma((1,)), dma((1,)),
    ]
    return pl.pallas_call(
        kernel,
        out_shape=jax.ShapeDtypeStruct((32, 256), BF),
        in_specs=[hb] * 16,
        out_specs=vm,
        scratch_shapes=scratch,
        name="decode_step",
        cost_estimate=pl.CostEstimate(flops=3_000_000_000, bytes_accessed=26_000_000, transcendentals=200_000),
        compiler_params=pltpu.CompilerParams(
            collective_id=0, has_side_effects=True, vmem_limit_bytes=56 * 2**20
        ),
    )(
        lengths, policy.reshape(8), retained_blocks.transpose(1, 2, 0).reshape(4, 8),
        queries, new_key.reshape(8, 128), incoming_value.reshape(8, 128),
        routes.T, router_logits.T, norm_gain.reshape(32, 128),
        key_cache.reshape(8, 1024, 128), stored_value_cache.reshape(8, 1024, 128),
        out_weight.reshape(32, 2, 128, 128), residual,
        gate_weight, up_weight, down_weight.reshape(768, 4096),
    ).T


def solution(mesh):
    return jax.shard_map(
        per_device,
        mesh=mesh,
        in_specs=(
            P("ep", "tp", None),
            P("ep", "tp", None, None),
            P("ep", "tp", None, None),
            P("ep", "tp", None),
            P("ep", "tp", None),
            P("ep"),
            P("ep", "tp"),
            P("ep", "tp", None),
            P(None, "ep"),
            P(None, "ep"),
            P(),
            P(),
            P(),
            P("ep", None, "tp"),
            P("ep", None, "tp"),
            P("ep", "tp", None),
        ),
        out_specs=P(None, ("ep", "tp")),
        check_vma=False,
    )
```

time: 78.1 us -> 61.1 us (0.78)
  the two profiles are of different devices: /device:TPU:8 before, /device:TPU:1 now
where the time goes in v2:
time: 61.1 us; the launch traced here: 60.6 us
  Pallas kernels  59.3 us (97%)
  local copies, waits for them, and re-layouts  1.32 us (2%)
    pallas_call x1, Pallas kernels, per_device(): pl.pallas_call(kernel, out_shape=jax.ShapeDtypeStruct((32, 256), BF), in_...  59.3 us
    unnamed x1, local copies, waits for them, and re-layouts  1.32 us

profile of v2, /device:TPU:1, one launch (start us, length us, event | category | flops | bytes accessed | tf_op | source)
XLA Modules:
  0.0 60.6 jit_solution(7586618256658529781)
XLA Ops:
  0.0 59.3 %decode_step.1 = bf16[32,256]{1,0:T(8,128)(2,1)} custom-call(s32[8]{0:T(128)} %len_hbm.1, s32[8]{0:T(128)} %bitcast.25, s32[4,8]{1,0:T(4,128)} %bitcast.22, bf16[8,16,128]{2,1,0:T(8,128)(2,1)} %q_hbm.1, bf16[8,128]{1,0:T(8,128)(2,1)} %bitcast.23, bf16[8,128]{1,0:T(8,128)(2,1)} %bitcast.24, s32[8,256]{1,0:T(8,128)} %bitcast.20, f32[8,256]{1,0:T(8,128)} %bitcast.21, ...), custom_call_target="tpu_custom_call" | custom-call | flops 3000000000 | bytes 26000000 | tf_op jit(solution)/shard_map/decode_step/pallas_call | solution.py:403
  59.3 1.3 %copy.18 = bf16[256,32]{0,1:T(8,128)(2,1)} copy(bf16[256,32]{0,1:T(8,128)(2,1)} %bitcast.18) | data formatting | bytes 32768

commit v3 on v2

--- a/solution.py
+++ b/solution.py
@@ -60,25 +60,31 @@
     def got(ref, sem):
         remote(ref, ref, sb.at[0], sem, sib).wait_recv()
 
+    def cache_copy(hbm, buf, sem, i):
+        return pltpu.make_async_copy(hbm.at[pl.ds(2 * i, 2)], buf.at[pl.ds(2 * i, 2)], sem.at[i])
+
+    smalls = [
+        pltpu.make_async_copy(src, dst, small.at[i])
+        for i, (src, dst) in enumerate((
+            (q_hbm, q_ref), (nk_hbm, nk_ref), (len_hbm, len_ref), (pol_hbm, pol_ref), (ret_hbm, ret_ref),
+            (nv_hbm, nv_ref), (routes_hbm, routes_ref), (logit_hbm, logit_ref), (gain_hbm, gain_ref),
+        ))
+    ]
+    cache_copy(k_hbm, kbuf, ksem, 0).start()
+    for cp in smalls[:5]:
+        cp.start()
+    for i in range(1, 4):
+        cache_copy(k_hbm, kbuf, ksem, i).start()
+
     bar = pltpu.get_barrier_semaphore()
     partners = [sib] + [peer(d, 0, 0) for d in near] + [peer(0, d, 0) for d in near] + [peer(0, 0, d) for d in near]
     for dev in partners:
         pl.semaphore_signal(bar, inc=1, device_id=dev, device_id_type=MESH)
 
-    smalls = [
-        pltpu.make_async_copy(src, dst, small.at[i])
-        for i, (src, dst) in enumerate((
-            (routes_hbm, routes_ref), (logit_hbm, logit_ref),
-            (len_hbm, len_ref), (pol_hbm, pol_ref), (ret_hbm, ret_ref),
-            (q_hbm, q_ref), (nk_hbm, nk_ref), (nv_hbm, nv_ref), (gain_hbm, gain_ref),
-        ))
-    ]
-    for cp in smalls:
+    for i in range(4):
+        cache_copy(v_hbm, vbuf, vsem, i).start()
+    for cp in smalls[5:]:
         cp.start()
-    for r in range(8):
-        pltpu.make_async_copy(k_hbm.at[r], kbuf.at[r], ksem.at[r]).start()
-    for r in range(8):
-        pltpu.make_async_copy(v_hbm.at[r], vbuf.at[r], vsem.at[r]).start()
     weights = [
         pltpu.make_async_copy(ow_hbm.at[pl.ds(8 * x, 8), 0], owb.at[:, :, pl.ds(0, 128)], wsem.at[0]),
         pltpu.make_async_copy(ow_hbm.at[pl.ds(8 * x, 8), 1], owb.at[:, :, pl.ds(128, 128)], wsem.at[1]),
@@ -90,9 +96,95 @@
         pltpu.make_async_copy(down_hbm, dn, wsem.at[7]),
     ]
 
-    for cp in smalls:
+    for cp in smalls[:5]:
         cp.wait()
 
+    scale = 128 ** (-0.5)
+    pos = lax.broadcasted_iota(jnp.int32, (1, 1024), 1)
+    blk = pos >> 6
+    for r in range(8):
+        length = len_ref[r]
+        pol = pol_ref[r]
+        used = (length + 63) >> 6
+        low = jnp.where(pol == 0, used - 2, jnp.where(pol == 2, 0, used - 1))
+        keep = blk >= low
+        for k in range(4):
+            named = jnp.where(pol == 1, ret_ref[k, r], -1)
+            keep = keep | (blk == named)
+        bias = jnp.where(keep & (pos < length), 0.0, -jnp.inf).astype(F32)
+        qr = q_ref[r]
+        own = jnp.sum(qr.astype(F32) * nk_ref[pl.ds(r, 1), :].astype(F32), axis=1, keepdims=True) * scale
+        if r % 2 == 0:
+            cache_copy(k_hbm, kbuf, ksem, r // 2).wait()
+        s = mm(qr, kbuf[r], ((1,), (1,))) * scale + bias
+        top = jnp.maximum(jnp.max(s, axis=1, keepdims=True), own)
+        p = jnp.exp(s - top)
+        ownw = jnp.exp(own - top)
+        pbuf[r] = p.astype(BF)
+        tbuf[r] = jnp.broadcast_to(jnp.sum(p, axis=1, keepdims=True) + ownw, (16, 128))
+        obuf[r] = jnp.broadcast_to(ownw, (16, 128)).astype(BF)
+    for w in weights[:3]:
+        w.start()
+    smalls[5].wait()
+    for r in range(8):
+        if r % 2 == 0:
+            cache_copy(v_hbm, vbuf, vsem, r // 2).wait()
+        o = mm(pbuf[r], vbuf[r])
+        o = o + obuf[r].astype(F32) * nv_ref[pl.ds(r, 1), :].astype(F32)
+        att[:, r, :] = o / tbuf[r]
+    for w in weights[3:]:
+        w.start()
+    here = 4 * a2 + a1
+    attg[c, here] = att[...].reshape(128, 128).astype(BF)
+
+    pl.semaphore_wait(bar, len(partners))
+
+    class Gather:
+        def __init__(self, buf, sends, gets, sib_sends, sib_gets):
+            self.buf, self.sends, self.gets = buf, sends, gets
+            self.sib_sends, self.sib_gets = sib_sends, sib_gets
+
+        def row(self, d2, cc):
+            base = a2 if cc is c else a1
+            return self.buf.at[cc, pl.ds(4 * ((base + 4 - d2) % 4), 4)]
+
+        def send(self, d1, get, dev):
+            at = self.buf.at[c, 4 * a2 + (a1 + 4 - d1) % 4]
+            remote(at, at, self.sends.at[0], self.gets.at[get], dev).start()
+
+        def over(self, d2):
+            at = self.row(d2, c)
+            remote(at, at, self.sib_sends.at[0], self.sib_gets.at[d2], sib).start()
+
+        def start(self):
+            for d in near:
+                self.send(0, 4 + d, over_axis1(d))
+            for d in near:
+                self.send(0, d, over_axis2(d))
+
+        def relay(self):
+            for d1 in near:
+                got(self.buf.at[c, 4 * a2 + (a1 + 4 - d1) % 4], self.gets.at[4 + d1])
+                for d2 in near:
+                    self.send(d1, d2, over_axis2(d2))
+            self.over(0)
+
+        def pass_on(self, d2):
+            got(self.row(d2, c), self.gets.at[d2])
+            self.over(d2)
+
+        def arrived(self, d2):
+            got(self.row(d2, 1 - c), self.sib_gets.at[d2])
+
+        def finish(self):
+            sent(self.buf.at[c, pl.ds(0, 15)], self.sends.at[0])
+            sent(self.buf.at[c], self.sib_sends.at[0])
+
+    attended = Gather(attg, sa, ra, sas, ras)
+    attended.start()
+
+    for cp in smalls[6:]:
+        cp.wait()
     logits = logit_ref[...]
     grown = jnp.exp(logits - jnp.max(logits, axis=0, keepdims=True))
     rw = grown / jnp.sum(grown, axis=0, keepdims=True)
@@ -118,89 +210,6 @@
         ptb[e] = jnp.where(inside, spread_t, 0.0).astype(BF)
         wcol[e] = jnp.broadcast_to(jnp.sum(jnp.where(inside, weight_t, 0.0), axis=1, keepdims=True), (256, 128))
 
-    scale = 128 ** (-0.5)
-    pos = lax.broadcasted_iota(jnp.int32, (1, 1024), 1)
-    blk = pos >> 6
-    for r in range(8):
-        length = len_ref[r]
-        pol = pol_ref[r]
-        used = (length + 63) >> 6
-        low = jnp.where(pol == 0, used - 2, jnp.where(pol == 2, 0, used - 1))
-        keep = blk >= low
-        for k in range(4):
-            named = jnp.where(pol == 1, ret_ref[k, r], -1)
-            keep = keep | (blk == named)
-        bias = jnp.where(keep & (pos < length), 0.0, -jnp.inf).astype(F32)
-        qr = q_ref[r]
-        own = jnp.sum(qr.astype(F32) * nk_ref[pl.ds(r, 1), :].astype(F32), axis=1, keepdims=True) * scale
-        pltpu.make_async_copy(k_hbm.at[r], kbuf.at[r], ksem.at[r]).wait()
-        s = mm(qr, kbuf[r], ((1,), (1,))) * scale + bias
-        top = jnp.maximum(jnp.max(s, axis=1, keepdims=True), own)
-        p = jnp.exp(s - top)
-        ownw = jnp.exp(own - top)
-        pbuf[r] = p.astype(BF)
-        tbuf[r] = jnp.broadcast_to(jnp.sum(p, axis=1, keepdims=True) + ownw, (16, 128))
-        obuf[r] = jnp.broadcast_to(ownw, (16, 128)).astype(BF)
-    for w in weights[:3]:
-        w.start()
-    for r in range(8):
-        pltpu.make_async_copy(v_hbm.at[r], vbuf.at[r], vsem.at[r]).wait()
-        o = mm(pbuf[r], vbuf[r])
-        o = o + obuf[r].astype(F32) * nv_ref[pl.ds(r, 1), :].astype(F32)
-        att[pl.ds(16 * r, 16), :] = (o / tbuf[r]).astype(BF)
-    for w in weights[3:]:
-        w.start()
-    rows = lax.broadcasted_iota(jnp.int32, (128, 128), 0)
-    cols = lax.broadcasted_iota(jnp.int32, (128, 128), 1)
-    perm = jnp.where(cols == (rows % 8) * 16 + rows // 8, 1.0, 0.0).astype(BF)
-    here = 4 * a2 + a1
-    attg[c, here] = mm(perm, att[...]).astype(BF)
-
-    pl.semaphore_wait(bar, len(partners))
-
-    class Gather:
-        def __init__(self, buf, sends, gets, sib_sends, sib_gets):
-            self.buf, self.sends, self.gets = buf, sends, gets
-            self.sib_sends, self.sib_gets = sib_sends, sib_gets
-
-        def row(self, d2, cc):
-            base = a2 if cc is c else a1
-            return self.buf.at[cc, pl.ds(4 * ((base + 4 - d2) % 4), 4)]
-
-        def send(self, d1, get, dev):
-            at = self.buf.at[c, 4 * a2 + (a1 + 4 - d1) % 4]
-            remote(at, at, self.sends.at[0], self.gets.at[get], dev).start()
-
-        def over(self, d2):
-            at = self.row(d2, c)
-            remote(at, at, self.sib_sends.at[0], self.sib_gets.at[d2], sib).start()
-
-        def start(self):
-            for d in near:
-                self.send(0, 4 + d, over_axis1(d))
-            for d in near:
-                self.send(0, d, over_axis2(d))
-
-        def relay(self):
-            for d1 in near:
-                got(self.buf.at[c, 4 * a2 + (a1 + 4 - d1) % 4], self.gets.at[4 + d1])
-                for d2 in near:
-                    self.send(d1, d2, over_axis2(d2))
-            self.over(0)
-
-        def pass_on(self, d2):
-            got(self.row(d2, c), self.gets.at[d2])
-            self.over(d2)
-
-        def arrived(self, d2):
-            got(self.row(d2, 1 - c), self.sib_gets.at[d2])
-
-        def finish(self):
-            sent(self.buf.at[c, pl.ds(0, 15)], self.sends.at[0])
-            sent(self.buf.at[c], self.sib_sends.at[0])
-
-    attended = Gather(attg, sa, ra, sas, ras)
-    attended.start()
     attended.relay()
     for d in near:
         attended.pass_on(d)
@@ -282,10 +291,12 @@
         spread = mm(ptb[e], act)
         aact[:, pl.ds(384 * e, 384)] = (spread * wcol[e][:, :1]).astype(BF)
 
+    def turn(i):
+        return jnp.where(i == 0, 2, jnp.where(i == 1, 1, jnp.where(i == 2, 3, 0)))
+
     def dest(n, cc):
-        i1 = n // 4
-        d1 = jnp.where(i1 == 0, 2, jnp.where(i1 == 1, 1, jnp.where(i1 == 2, 3, 0)))
-        d2 = n % 4
+        d1 = jnp.where(n < 12, turn(n % 3), 0)
+        d2 = turn(jnp.where(n < 12, n // 3, n - 12))
         dy = d1 * (1 - cc) + d2 * cc
         dz = d2 * (1 - cc) + d1 * cc
         return d1, d2, (y + dy) % 4 * 4 + (z + dz) % 4
@@ -306,8 +317,7 @@
     def forward(n):
         d1, d2, _ = dest(n, c)
         qbuf[n] = join(n).astype(BF)
-        to = r1.at[d2, n // 4]
-        remote(qbuf.at[n], to, sd1.at[0], rd1.at[d2], peer(0, d1 * (1 - c), d1 * c)).start()
+        remote(qbuf.at[n], r1.at[d2, n % 3], sd1.at[0], rd1.at[d2], peer(0, d1 * (1 - c), d1 * c)).start()
 
     down(0)
 
@@ -324,8 +334,8 @@
     def slab(j):
         return pl.ds(pl.multiple_of(32 * (j % 4), 32), 32)
 
-    for d2 in (2, 1, 3, 0):
-        total = join(12 + d2)
+    for i2, d2 in enumerate((2, 1, 3, 0)):
+        total = join(12 + i2)
         got(r1.at[d2], rd1.at[d2])
         for i1 in range(3):
             total = total + r1[d2, i1].astype(F32)
@@ -369,7 +379,7 @@
         pltpu.VMEM((8, 16, 1024), BF),
         pltpu.VMEM((8, 16, 128), F32),
         pltpu.VMEM((8, 16, 128), BF),
-        pltpu.VMEM((128, 128), BF),
+        pltpu.VMEM((16, 8, 128), F32),
         pltpu.VMEM((2, 16, 128, 128), BF),
         pltpu.VMEM((8, 128, 256), BF),
         pltpu.VMEM((4, 2, 128, 128), BF),
@@ -393,7 +403,7 @@
         pltpu.VMEM((32, 256), F32),
         pltpu.VMEM((128, 256), F32),
         pltpu.VMEM((16, 32, 256), BF),
-        dma((9,)), dma((8,)), dma((8,)), dma((8,)),
+        dma((9,)), dma((4,)), dma((4,)), dma((8,)),
         dma((1,)), dma((8,)), dma((1,)), dma((4,)),
         dma((1,)), dma((8,)),
         dma((1,)), dma((8,)), dma((1,)), dma((4,)),

time: 61.1 us -> 57.3 us (0.938)
  Pallas kernels: 59.3 us -> 55.4 us
    pallas_call x1, Pallas kernels: 59.3 us -> 55.4 us  [per_device(): pl.pallas_call(kernel, out_shape=jax.ShapeDtypeStruct((32, 256), BF), in_...]
where the time goes in v3:
time: 57.3 us; the launch traced here: 56.8 us
  Pallas kernels  55.4 us (97%)
  local copies, waits for them, and re-layouts  1.32 us (2%)
    pallas_call x1, Pallas kernels, per_device(): pl.pallas_call(kernel, out_shape=jax.ShapeDtypeStruct((32, 256), BF), in_...  55.4 us
    unnamed x1, local copies, waits for them, and re-layouts  1.32 us

profile of v3, /device:TPU:1, one launch (start us, length us, event | category | flops | bytes accessed | tf_op | source)
XLA Modules:
  0.0 56.8 jit_solution(16719076073805986386)
XLA Ops:
  0.0 55.4 %decode_step.1 = bf16[32,256]{1,0:T(8,128)(2,1)} custom-call(s32[8]{0:T(128)} %len_hbm.1, s32[8]{0:T(128)} %bitcast.25, s32[4,8]{1,0:T(4,128)} %bitcast.22, bf16[8,16,128]{2,1,0:T(8,128)(2,1)} %q_hbm.1, bf16[8,128]{1,0:T(8,128)(2,1)} %bitcast.23, bf16[8,128]{1,0:T(8,128)(2,1)} %bitcast.24, s32[8,256]{1,0:T(8,128)} %bitcast.20, f32[8,256]{1,0:T(8,128)} %bitcast.21, ...), custom_call_target="tpu_custom_call" | custom-call | flops 3000000000 | bytes 26000000 | tf_op jit(solution)/shard_map/decode_step/pallas_call | solution.py:413
  55.4 1.3 %copy.18 = bf16[256,32]{0,1:T(8,128)(2,1)} copy(bf16[256,32]{0,1:T(8,128)(2,1)} %bitcast.18) | data formatting | bytes 32768

commit v4 on v3

--- a/solution.py
+++ b/solution.py
@@ -9,6 +9,7 @@
 TOPK = 8
 CAP = 64
 EPSILON = 1e-06
+LAG = 4
 MESH = pl.DeviceIdType.MESH
 BF = jnp.bfloat16
 F32 = jnp.float32
@@ -319,15 +320,16 @@
         qbuf[n] = join(n).astype(BF)
         remote(qbuf.at[n], r1.at[d2, n % 3], sd1.at[0], rd1.at[d2], peer(0, d1 * (1 - c), d1 * c)).start()
 
-    down(0)
+    for n in range(LAG):
+        down(n)
 
     def step(n, _):
         down(n)
-        forward(n - 1)
+        forward(n - LAG)
         return 0
 
-    lax.fori_loop(1, 13, step, 0)
-    for n in range(13, 16):
+    lax.fori_loop(LAG, 12 + LAG, step, 0)
+    for n in range(12 + LAG, 16):
         down(n)
     hidden.finish()
 

time: 57.3 us -> 55.1 us (0.962)
  Pallas kernels: 55.4 us -> 53.6 us
    pallas_call x1, Pallas kernels: 55.4 us -> 53.6 us  [per_device(): pl.pallas_call(kernel, out_shape=jax.ShapeDtypeStruct((32, 256), BF), in_...]
where the time goes in v4:
time: 55.1 us; the launch traced here: 54.9 us
  Pallas kernels  53.6 us (97%)
  local copies, waits for them, and re-layouts  1.32 us (2%)
    pallas_call x1, Pallas kernels, per_device(): pl.pallas_call(kernel, out_shape=jax.ShapeDtypeStruct((32, 256), BF), in_...  53.6 us
    unnamed x1, local copies, waits for them, and re-layouts  1.32 us

profile of v4, /device:TPU:1, one launch (start us, length us, event | category | flops | bytes accessed | tf_op | source)
XLA Modules:
  0.0 54.9 jit_solution(5256903395926390572)
XLA Ops:
  0.0 53.6 %decode_step.1 = bf16[32,256]{1,0:T(8,128)(2,1)} custom-call(s32[8]{0:T(128)} %len_hbm.1, s32[8]{0:T(128)} %bitcast.25, s32[4,8]{1,0:T(4,128)} %bitcast.22, bf16[8,16,128]{2,1,0:T(8,128)(2,1)} %q_hbm.1, bf16[8,128]{1,0:T(8,128)(2,1)} %bitcast.23, bf16[8,128]{1,0:T(8,128)(2,1)} %bitcast.24, s32[8,256]{1,0:T(8,128)} %bitcast.20, f32[8,256]{1,0:T(8,128)} %bitcast.21, ...), custom_call_target="tpu_custom_call" | custom-call | flops 3000000000 | bytes 26000000 | tf_op jit(solution)/shard_map/decode_step/pallas_call | solution.py:415
  53.6 1.3 %copy.18 = bf16[256,32]{0,1:T(8,128)(2,1)} copy(bf16[256,32]{0,1:T(8,128)(2,1)} %bitcast.18) | data formatting | bytes 32768

commit v5 on v4

--- a/solution.py
+++ b/solution.py
@@ -161,18 +161,24 @@
             for d in near:
                 self.send(0, 4 + d, over_axis1(d))
             for d in near:
-                self.send(0, d, over_axis2(d))
+                self.send(0, d if d != 2 else 8, over_axis2(d))
 
         def relay(self):
             for d1 in near:
                 got(self.buf.at[c, 4 * a2 + (a1 + 4 - d1) % 4], self.gets.at[4 + d1])
                 for d2 in near:
-                    self.send(d1, d2, over_axis2(d2))
+                    self.send(d1, d2 if d2 != 2 else 8 + d1, over_axis2(d2))
             self.over(0)
 
         def pass_on(self, d2):
-            got(self.row(d2, c), self.gets.at[d2])
-            self.over(d2)
+            if d2 != 2:
+                got(self.row(d2, c), self.gets.at[d2])
+                self.over(d2)
+                return
+            for d1 in (0,) + near:
+                at = self.buf.at[c, 4 * ((a2 + 2) % 4) + (a1 + 4 - d1) % 4]
+                got(at, self.gets.at[8 + d1])
+                remote(at, at, self.sib_sends.at[0], self.sib_gets.at[d2], sib).start()
 
         def arrived(self, d2):
             got(self.row(d2, 1 - c), self.sib_gets.at[d2])
@@ -230,9 +236,17 @@
             remote(pb.at[x, cc], pb.at[x, cc], sb.at[0], rb.at[2 * d + half], peer(d, 0, 0)).start()
 
     project(c, 0)
-    for d in (0,) + near:
-        attended.arrived(d)
-    project(1 - c, 1)
+    for d2 in (0,) + near:
+        attended.arrived(d2)
+        row = (a1 + 4 - d2) % 4
+        total = jnp.zeros((64, 256), F32)
+        for g in range(8):
+            total = total + mm(attg[1 - c, pl.ds(4 * row, 4), pl.ds(16 * g, 16), :].reshape(64, 128), owb[g])
+        total = total.reshape(4, 16, 256)
+        total = total[:, :8, :128] + total[:, 8:, 128:]
+        pb[x, 1 - c, pl.ds(pl.multiple_of(32 * row, 32), 32), :] = total.reshape(32, 128).astype(BF)
+    for d in near:
+        remote(pb.at[x, 1 - c], pb.at[x, 1 - c], sb.at[0], rb.at[2 * d + 1], peer(d, 0, 0)).start()
     attended.finish()
     weights[2].wait()
     for half, cc in ((0, c), (1, 1 - c)):
@@ -406,9 +420,9 @@
         pltpu.VMEM((128, 256), F32),
         pltpu.VMEM((16, 32, 256), BF),
         dma((9,)), dma((4,)), dma((4,)), dma((8,)),
-        dma((1,)), dma((8,)), dma((1,)), dma((4,)),
+        dma((1,)), dma((12,)), dma((1,)), dma((4,)),
         dma((1,)), dma((8,)),
-        dma((1,)), dma((8,)), dma((1,)), dma((4,)),
+        dma((1,)), dma((12,)), dma((1,)), dma((4,)),
         dma((1,)), dma((16,)), dma((1,)), dma((4,)),
         dma((1,)), dma((1,)),
     ]

time: 55.1 us -> 54.9 us (level)
  Pallas kernels: 53.6 us -> 52.9 us
    pallas_call x1, Pallas kernels: 53.6 us -> 52.9 us  [per_device(): pl.pallas_call(kernel, out_shape=jax.ShapeDtypeStruct((32, 256), BF), in_...]
where the time goes in v5:
time: 54.9 us; the launch traced here: 54.2 us
  Pallas kernels  52.9 us (96%)
  local copies, waits for them, and re-layouts  1.32 us (2%)
    pallas_call x1, Pallas kernels, per_device(): pl.pallas_call(kernel, out_shape=jax.ShapeDtypeStruct((32, 256), BF), in_...  52.9 us
    unnamed x1, local copies, waits for them, and re-layouts  1.32 us

profile of v5, /device:TPU:1, one launch (start us, length us, event | category | flops | bytes accessed | tf_op | source)
XLA Modules:
  0.0 54.2 jit_solution(6462328685705322916)
XLA Ops:
  0.0 52.9 %decode_step.1 = bf16[32,256]{1,0:T(8,128)(2,1)} custom-call(s32[8]{0:T(128)} %len_hbm.1, s32[8]{0:T(128)} %bitcast.25, s32[4,8]{1,0:T(4,128)} %bitcast.22, bf16[8,16,128]{2,1,0:T(8,128)(2,1)} %q_hbm.1, bf16[8,128]{1,0:T(8,128)(2,1)} %bitcast.23, bf16[8,128]{1,0:T(8,128)(2,1)} %bitcast.24, s32[8,256]{1,0:T(8,128)} %bitcast.20, f32[8,256]{1,0:T(8,128)} %bitcast.21, ...), custom_call_target="tpu_custom_call" | custom-call | flops 3000000000 | bytes 26000000 | tf_op jit(solution)/shard_map/decode_step/pallas_call | solution.py:429
  52.9 1.3 %copy.18 = bf16[256,32]{0,1:T(8,128)(2,1)} copy(bf16[256,32]{0,1:T(8,128)(2,1)} %bitcast.18) | data formatting | bytes 32768
